TPU v7x, 32 devices: a whole 2x2x4 slice. The times are simulated.
32 devices in a mesh: gx: 8 (over y, x, core), gy: 4 (over z).
Axes of the slice: x: 2, y: 2, z: 4, core: 2. Of those that a mesh axis runs over, the one named last changes fastest.
Arguments:
- concentration: bfloat16 [128, 128, 512], P(None, 'gx', 'gy'), may hold values from 0.099609375 to 1
- adjoint_next: bfloat16 [128, 128, 512], P(None, 'gx', 'gy'), may hold values from 0 to 2
- sign_x: int32 [128, 512], P('gx', 'gy'), may hold values from 0 to 1
- sign_y: int32 [128, 512], P('gx', 'gy'), may hold values from 0 to 1
- courant_x: float32 [128, 512], P('gx', 'gy'), may hold values from 0.05 to 0.24
- courant_y: float32 [128, 512], P('gx', 'gy'), may hold values from 0.05 to 0.24
- active: int32 [128, 512], P('gx', 'gy'), may hold values from 0 to 1, as said below
- kernel_a: float32 [128], replicated, may hold values from 0.01 to 0.1
- kernel_b: float32 [128], replicated, may hold values from 0.01 to 0.1
Outputs:
- gradient: float32 [128, 128, 512], P(None, 'gx', 'gy')
Inputs may be any that keep to these rules, and one draw needn't show every extreme that they name: Among the devices that share one gy index, 2 hold exactly 2048 active cells (all of their cells) and the others exactly 256; which devices hold more is drawn anew.
All inputs are finite; a program needn't handle non-finite values.
Results may differ from a plain program's by a relative error of at most 0.0003.
Values sent between devices are 32-bit elements; how exact they have to be, the bound alone decides.
A program may use at most 64 MiB of HBM per device.

v0:
```python
import functools

import jax
import jax.numpy as jnp
import numpy as np
from jax import lax
from jax.experimental import pallas as pl
from jax.experimental.pallas import tpu as pltpu
from jax.sharding import PartitionSpec as P

SUBSTEPS = 4
F32 = jnp.float32
BF16 = jnp.bfloat16


def dft_tables(bins):
    freq = 2 * np.arange(bins) + 1
    index = np.arange(bins)
    angle = np.pi * (freq[:, None] * index[None, :] % (4 * bins)) / (2 * bins)
    forward = np.concatenate([np.cos(angle), -np.sin(angle)], axis=0)

    def inverse(outputs):
        phase = np.pi * (outputs[:, None] * freq[None, :] % (4 * bins)) / (2 * bins)
        return np.concatenate([np.cos(phase), -np.sin(phase)], axis=1) / bins

    gain = inverse(index - 1) * (index > 0)[:, None]
    lag = inverse(index + 1)
    return tuple(np.asarray(t, np.float32) for t in (forward, gain, lag))


def split(values):
    high = values.astype(BF16)
    low = (values - high.astype(F32)).astype(BF16)
    return high, low


def stacked(values):
    high, low = split(values)
    return jnp.concatenate([high, low, high], axis=0)


def table3(values):
    high, low = split(values)
    return jnp.concatenate([high, high, low], axis=1)


def dot(table, values):
    return jnp.dot(table, values, preferred_element_type=F32)


def product(left, right):
    half = left.shape[0] // 2
    lr, li, rr, ri = left[:half], left[half:], right[:half], right[half:]
    return jnp.concatenate([lr * rr - li * ri, lr * ri + li * rr], axis=0)


def product_conj(left, right):
    half = left.shape[0] // 2
    lr, li, rr, ri = left[:half], left[half:], right[:half], right[half:]
    return jnp.concatenate([lr * rr + li * ri, li * rr - lr * ri], axis=0)


def kernel(
    n_gx, n_gy, width_x,
    *refs,
):
    inputs, refs = refs[:12], refs[12:]
    out, refs = refs[0], refs[1:]
    fetched, refs = refs[:12], refs[12:]
    conc, adj, sx, sy, cx, cy, active, ka_ref, kb_ref, fwd_ref, gain_ref, lag_ref = fetched
    (wide, wide_adj, state, lam, y_send, y_recv, z_send, z_recv, moved, faces, t_fwd, t_gain, t_lam, t_lag,
     send_sem, recv_sem, in_sem) = refs
    fetches = [pltpu.make_async_copy(i, f, in_sem.at[k]) for k, (i, f) in enumerate(zip(inputs, fetched))]
    for k in (0, 2, 3, 4, 5, 1, 7, 8, 9, 10, 11, 6):
        fetches[k].start()
    bins = ka_ref.shape[1]
    width_y = sx.shape[1]
    gx = lax.axis_index("gx")
    gy = lax.axis_index("gy")
    nxt_x, prv_x = lax.rem(gx + 1, n_gx), lax.rem(gx + n_gx - 1, n_gx)
    nxt_y, prv_y = jnp.minimum(gy + 1, n_gy - 1), jnp.maximum(gy - 1, 0)
    has_prv, has_nxt = gy > 0, gy < n_gy - 1
    mesh_id = pl.DeviceIdType.MESH

    barrier = pltpu.get_barrier_semaphore()
    pl.semaphore_signal(barrier, inc=1, device_id=(prv_x, gy), device_id_type=mesh_id)
    pl.semaphore_signal(barrier, inc=1, device_id=(nxt_x, gy), device_id_type=mesh_id)

    @pl.when(has_prv)
    def _():
        pl.semaphore_signal(barrier, inc=1, device_id=(gx, prv_y), device_id_type=mesh_id)

    @pl.when(has_nxt)
    def _():
        pl.semaphore_signal(barrier, inc=1, device_id=(gx, nxt_y), device_id_type=mesh_id)

    lane = lax.broadcasted_iota(jnp.int32, (bins, width_y), 1)
    lane_x = lax.broadcasted_iota(jnp.int32, (width_x, width_y), 1)

    for k in (2, 3, 4, 5):
        fetches[k].wait()
    plus_x = sx[...].astype(F32)
    plus_y = sy[...].astype(F32)
    inside = (lane_x + gy * width_y > 0).astype(F32)
    ux = cx[...] * plus_x
    bx = cx[...] * (1.0 - plus_x)
    uy = cy[...] * plus_y * inside
    by = cy[...] * (1.0 - plus_y) * inside

    fetches[0].wait()
    wide[...] = conc[...].astype(F32)
    for x in (0, width_x - 1):
        state[x + 1, :bins, :] = wide[pl.ds(x, bins, stride=width_x), :]
    state[1, bins:bins + 1, :] = ux[0:1]
    state[1, bins + 1:bins + 2, :] = bx[0:1]
    state[1, bins + 2:, :] = jnp.zeros((6, width_y), F32)
    state[width_x, bins:, :] = jnp.zeros((8, width_y), F32)

    def x_copies(field, base):
        return (
            pltpu.make_async_remote_copy(
                src_ref=field.at[1], dst_ref=field.at[width_x + 1],
                send_sem=send_sem.at[base], recv_sem=recv_sem.at[base],
                device_id=(prv_x, gy), device_id_type=mesh_id),
            pltpu.make_async_remote_copy(
                src_ref=field.at[width_x], dst_ref=field.at[0],
                send_sem=send_sem.at[base + 1], recv_sem=recv_sem.at[base + 1],
                device_id=(nxt_x, gy), device_id_type=mesh_id),
        )

    pl.semaphore_wait(barrier, 2 + has_prv.astype(jnp.int32) + has_nxt.astype(jnp.int32))
    first_x = x_copies(state, 0)
    for copy in first_x:
        copy.start()
    for x in range(1, width_x - 1):
        state[x + 1, :bins, :] = wide[pl.ds(x, bins, stride=width_x), :]

    def edges(field, places):
        to_prv = jnp.zeros((bins, width_y), F32)
        to_nxt = jnp.zeros((bins, width_y), F32)
        for x in places:
            slab = field[x + 1, :bins, :]
            to_prv = jnp.where(lane == x, pltpu.roll(slab, x, 1), to_prv)
            to_nxt = jnp.where(lane == x, pltpu.roll(slab, x + 1, 1), to_nxt)
        return to_prv, to_nxt

    y_send[0, :bins, :], y_send[1, :bins, :] = edges(state, range(width_x))
    y_send[0, bins:bins + width_x, :] = uy
    y_send[0, bins + width_x:, :] = by
    y_send[1, bins:, :] = jnp.zeros((2 * width_x, width_y), F32)

    def y_copies(source, target, base):
        return (
            pltpu.make_async_remote_copy(
                src_ref=source.at[0], dst_ref=target.at[1],
                send_sem=send_sem.at[base], recv_sem=recv_sem.at[base],
                device_id=(gx, prv_y), device_id_type=mesh_id),
            pltpu.make_async_remote_copy(
                src_ref=source.at[1], dst_ref=target.at[0],
                send_sem=send_sem.at[base + 1], recv_sem=recv_sem.at[base + 1],
                device_id=(gx, nxt_y), device_id_type=mesh_id),
        )

    def start_y(copies, target):
        to_prv, to_nxt = copies

        @pl.when(has_prv)
        def _():
            to_prv.start()

        @pl.when(has_nxt)
        def _():
            to_nxt.start()

        @pl.when(jnp.logical_not(has_prv))
        def _():
            target[0] = jnp.zeros(target.shape[1:], F32)

        @pl.when(jnp.logical_not(has_nxt))
        def _():
            target[1] = jnp.zeros(target.shape[1:], F32)

    def wait_y(copies):
        to_prv, to_nxt = copies

        @pl.when(has_prv)
        def _():
            to_prv.wait_send()
            to_nxt.wait_recv()

        @pl.when(has_nxt)
        def _():
            to_nxt.wait_send()
            to_prv.wait_recv()

    first_y = y_copies(y_send, y_recv, 2)
    start_y(first_y, y_recv)

    for k in (7, 8, 9, 10, 11):
        fetches[k].wait()
    ka_row, kb_row = ka_ref[...], kb_ref[...]
    ka_full = jnp.broadcast_to(ka_row, (bins, bins))
    kb_full = jnp.broadcast_to(kb_row, (bins, bins))
    ka_col, kb_col = ka_full.T, kb_full.T
    pair = ka_col * kb_full + kb_col * ka_full
    forward = fwd_ref[...]
    t_fwd[0:2 * bins, :] = table3(forward * ka_row)
    t_fwd[2 * bins:4 * bins, :] = table3(forward * kb_row)
    t_fwd[4 * bins:, :] = table3(pair)
    t_gain[...] = table3(gain_ref[...])
    t_lam[...] = table3(forward)
    lag = lag_ref[...]
    ka_col2 = jnp.concatenate([ka_col, ka_col], axis=1)
    kb_col2 = jnp.concatenate([kb_col, kb_col], axis=1)
    t_lag[:, :6 * bins] = table3(ka_col2 * lag)
    t_lag[:, 6 * bins:12 * bins] = table3(kb_col2 * lag)
    t_lag[:, 12 * bins:] = table3(-pair)

    fetches[1].wait()
    fetches[6].wait()
    wide_adj[...] = adj[...].astype(F32)
    for x in range(width_x):
        lam[x + 1, :bins, :] = wide_adj[pl.ds(x, bins, stride=width_x), :]

    wait_y(first_y)
    for copy in first_x:
        copy.wait()

    ux_next = jnp.concatenate([ux[1:], state[width_x + 1, bins:bins + 1, :]], axis=0)
    bx_next = jnp.concatenate([bx[1:], state[width_x + 1, bins + 1:bins + 2, :]], axis=0)
    last_lane = lane_x == width_y - 1
    uy_next = jnp.where(
        last_lane, pltpu.roll(y_recv[1, bins:bins + width_x, :], width_y - 1, 1), pltpu.roll(uy, width_y - 1, 1))
    by_next = jnp.where(
        last_lane, pltpu.roll(y_recv[1, bins + width_x:, :], width_y - 1, 1), pltpu.roll(by, width_y - 1, 1))
    centre = 1.0 - bx - ux_next - by - uy_next
    for index, values in enumerate((centre, ux, bx, ux_next, bx_next, uy, by, uy_next, by_next)):
        faces[index] = values

    def stencil(field, halo, x, low_x, high_x, low_y, high_y):
        slab = field[x + 1, :bins, :]
        before = jnp.where(lane == 0, pltpu.roll(halo[0, :bins, :], (width_y - x) % width_y, 1), pltpu.roll(slab, 1, 1))
        after = jnp.where(
            lane == width_y - 1, pltpu.roll(halo[1, :bins, :], width_y - 1 - x, 1), pltpu.roll(slab, width_y - 1, 1))
        row = lambda k: faces[k, x:x + 1, :]
        return (
            slab * row(0)
            + row(low_x) * field[x, :bins, :]
            + row(high_x) * field[x + 2, :bins, :]
            + row(low_y) * before
            + row(high_y) * after
        )

    for x in range(width_x):
        moved[x] = stencil(state, y_recv, x, 1, 4, 5, 8)

    lam[1, bins:, :] = jnp.zeros((8, width_y), F32)
    lam[width_x, bins:, :] = jnp.zeros((8, width_y), F32)
    half, quarter = width_x // 2, width_x // 4
    second_x = x_copies(lam, 4)

    def second_y(group):
        return y_copies(z_send.at[group], z_recv.at[group], 6 + 2 * group)

    @pl.loop(0, 2)
    def _(group):
        places = [p + quarter * group for p in range(quarter)]
        places += [p + half - quarter * group for p in range(quarter, half)]
        current = jnp.concatenate([moved[x] for x in places], axis=1)
        start = jnp.concatenate([lam[x + 1, :bins, :] for x in places], axis=1)
        saved = []
        for step in range(SUBSTEPS):
            spectra = dot(t_fwd[...], stacked(current))
            loss = spectra[4 * bins:]
            saved.append((current, spectra, loss))
            if step < SUBSTEPS - 1:
                both = product(spectra[:2 * bins], spectra[2 * bins:4 * bins])
                current = current + dot(t_gain[...], stacked(both)) - current * loss
        adjoint = start
        for step in reversed(range(SUBSTEPS)):
            current, spectra, loss = saved[step]
            spectra_l = dot(t_lam[...], stacked(adjoint))
            with_b = product_conj(spectra_l, spectra[2 * bins:4 * bins])
            with_a = product_conj(spectra_l, spectra[:2 * bins])
            terms = jnp.concatenate([stacked(with_b), stacked(with_a), stacked(adjoint * current)], axis=0)
            adjoint = adjoint + dot(t_lag[...], terms) - adjoint * loss
        on = jnp.concatenate([active[pl.ds(x, 1), :] for x in places], axis=1) == 1
        result = jnp.where(on, adjoint, start)
        for index, x in enumerate(places):
            lam[x + 1, :bins, :] = result[:, index * width_y:(index + 1) * width_y]

        @pl.when(group == 0)
        def _():
            for copy in second_x:
                copy.start()

        z_send[group, 0], z_send[group, 1] = edges(lam, places)
        start_y(second_y(group), z_recv.at[group])

    outer = [*range(quarter), *range(half + quarter, width_x)]
    for copy in second_x:
        copy.wait()
    for group, places in enumerate((outer, range(quarter, half + quarter))):
        wait_y(second_y(group))
        for x in places:
            out[pl.ds(x, bins, stride=width_x), :] = stencil(lam, z_recv.at[group], x, 2, 3, 6, 7)


def body(n_gx, n_gy, concentration, adjoint_next, sign_x, sign_y, courant_x, courant_y, active, kernel_a, kernel_b):
    bins, width_x, width_y = concentration.shape
    rows = bins * width_x
    tables = dft_tables(bins)
    operands = (
        concentration.reshape(rows, width_y),
        adjoint_next.reshape(rows, width_y),
        sign_x, sign_y, courant_x, courant_y, active,
        kernel_a.reshape(1, bins), kernel_b.reshape(1, bins),
        *(jnp.asarray(t) for t in tables),
    )
    result = pl.pallas_call(
        functools.partial(kernel, n_gx, n_gy, width_x),
        out_shape=pltpu.VMEM((rows, width_y), F32),
        in_specs=[pl.BlockSpec(memory_space=pltpu.HBM)] * 12,
        out_specs=pl.BlockSpec(memory_space=pltpu.VMEM),
        scratch_shapes=[
            *(pltpu.VMEM(a.shape, a.dtype) for a in operands),
            pltpu.VMEM((rows, width_y), F32),
            pltpu.VMEM((rows, width_y), F32),
            pltpu.VMEM((width_x + 2, bins + 8, width_y), F32),
            pltpu.VMEM((width_x + 2, bins + 8, width_y), F32),
            pltpu.VMEM((2, bins + 2 * width_x, width_y), F32),
            pltpu.VMEM((2, bins + 2 * width_x, width_y), F32),
            pltpu.VMEM((2, 2, bins, width_y), F32),
            pltpu.VMEM((2, 2, bins, width_y), F32),
            pltpu.VMEM((width_x, bins, width_y), F32),
            pltpu.VMEM((9, width_x, width_y), F32),
            pltpu.VMEM((5 * bins, 3 * bins), BF16),
            pltpu.VMEM((bins, 6 * bins), BF16),
            pltpu.VMEM((2 * bins, 3 * bins), BF16),
            pltpu.VMEM((bins, 15 * bins), BF16),
            pltpu.SemaphoreType.DMA((10,)),
            pltpu.SemaphoreType.DMA((10,)),
            pltpu.SemaphoreType.DMA((12,)),
        ],
        compiler_params=pltpu.CompilerParams(
            collective_id=0, has_side_effects=True, vmem_limit_bytes=60 * 1024 * 1024
        ),
    )(*operands)
    return result.reshape(bins, width_x, width_y)


def solution(mesh):
    return jax.shard_map(
        functools.partial(body, mesh.shape["gx"], mesh.shape["gy"]),
        mesh=mesh,
        in_specs=(
            P(None, "gx", "gy"),
            P(None, "gx", "gy"),
            P("gx", "gy"),
            P("gx", "gy"),
            P("gx", "gy"),
            P("gx", "gy"),
            P("gx", "gy"),
            P(),
            P(),
        ),
        out_specs=P(None, "gx", "gy"),
        check_vma=False,
    )
```

profile of v0, /device:TPU:0, one launch (start us, length us, event | category | flops | bytes accessed | tf_op | source)
XLA Modules:
  0.0 33.2 jit_solution(7866193727101135835)
XLA Ops:
  0.0 32.2 %shard_map.118 = f32[2048,128]{1,0:T(8,128)S(1)} custom-call(bf16[2048,128]{1,0:T(8,128)(2,1)} %bitcast.6, bf16[2048,128]{1,0:T(8,128)(2,1)} %bitcast.7, s32[16,128]{1,0:T(8,128)} %refs_2_.1, s32[16,128]{1,0:T(8,128)} %refs_3_.1, f32[16,128]{1,0:T(8,128)} %refs_4_.1, f32[16,128]{1,0:T(8,128)} %refs_5_.1, s32[16,128]{1,0:T(8,128)} %refs_6_.1, ...), custom_call_target="tpu_custom_call" | custom-call | tf_op jit(solution)/shard_map/pallas_call | solution.py:320
  32.2 1.0 %copy.14 = f32[128,16,128]{2,1,0:T(8,128)} copy(f32[128,16,128]{2,1,0:T(8,128)S(1)} %bitcast.5) | data formatting | bytes 2097152
where the time goes:
time: 33.3 us; the launch traced here: 33.2 us
  Pallas kernels  32.2 us (97%)
  local copies, waits for them, and re-layouts  0.97 us (3%)
    pallas_call x1, Pallas kernels, body(): pl.pallas_call(functools.partial(kernel, n_gx, n_gy, width_x), out_shape=...  32.2 us
    unnamed x1, local copies, waits for them, and re-layouts  0.97 us

commit v1 on v0

--- a/solution.py
+++ b/solution.py
@@ -9,22 +9,31 @@
 from jax.sharding import PartitionSpec as P
 
 SUBSTEPS = 4
+PART = 16
+BLOCK = 8
 F32 = jnp.float32
 BF16 = jnp.bfloat16
 
 
 def dft_tables(bins):
-    freq = 2 * np.arange(bins) + 1
+    order = np.arange(bins)
+    order = np.concatenate([order[:PART // 2], order[-(PART // 2):], order[PART // 2:-(PART // 2)]])
+    freq = 2 * order + 1
     index = np.arange(bins)
+
+    def chunked(real, imag):
+        pieces = [t[c:c + PART] for c in range(0, bins, PART) for t in (real, imag)]
+        return np.concatenate(pieces, axis=0)
+
     angle = np.pi * (freq[:, None] * index[None, :] % (4 * bins)) / (2 * bins)
-    forward = np.concatenate([np.cos(angle), -np.sin(angle)], axis=0)
+    forward = chunked(np.cos(angle), -np.sin(angle))
 
     def inverse(outputs):
-        phase = np.pi * (outputs[:, None] * freq[None, :] % (4 * bins)) / (2 * bins)
-        return np.concatenate([np.cos(phase), -np.sin(phase)], axis=1) / bins
+        phase = np.pi * (freq[:, None] * outputs[None, :] % (4 * bins)) / (2 * bins)
+        return chunked(np.cos(phase), -np.sin(phase)).T / bins
 
     gain = inverse(index - 1) * (index > 0)[:, None]
-    lag = inverse(index + 1)
+    lag = inverse(index + 1) - inverse(0 * index)
     return tuple(np.asarray(t, np.float32) for t in (forward, gain, lag))
 
 
@@ -34,30 +43,29 @@
     return high, low
 
 
-def stacked(values):
-    high, low = split(values)
-    return jnp.concatenate([high, low, high], axis=0)
-
-
-def table3(values):
-    high, low = split(values)
-    return jnp.concatenate([high, high, low], axis=1)
-
-
 def dot(table, values):
     return jnp.dot(table, values, preferred_element_type=F32)
 
 
-def product(left, right):
-    half = left.shape[0] // 2
-    lr, li, rr, ri = left[:half], left[half:], right[:half], right[half:]
-    return jnp.concatenate([lr * rr - li * ri, lr * ri + li * rr], axis=0)
-
-
-def product_conj(left, right):
-    half = left.shape[0] // 2
-    lr, li, rr, ri = left[:half], left[half:], right[:half], right[half:]
-    return jnp.concatenate([lr * rr + li * ri, li * rr - lr * ri], axis=0)
+def rows(*values):
+    return jnp.concatenate(values, axis=0)
+
+
+def product(ar, ai, br, bi):
+    return rows(ar * br - ai * bi, ar * bi + ai * br)
+
+
+def product_conj(lr, li, vr, vi):
+    return rows(lr * vr + li * vi, li * vr - lr * vi)
+
+
+def quarters(chunk):
+    return tuple(chunk[q * PART:(q + 1) * PART] for q in range(chunk.shape[0] // PART))
+
+
+def high_low(chunks):
+    high, low = split(chunks[0])
+    return [high, *(c.astype(BF16) for c in chunks[1:])], low
 
 
 def kernel(
@@ -68,7 +76,7 @@
     out, refs = refs[0], refs[1:]
     fetched, refs = refs[:12], refs[12:]
     conc, adj, sx, sy, cx, cy, active, ka_ref, kb_ref, fwd_ref, gain_ref, lag_ref = fetched
-    (wide, wide_adj, state, lam, y_send, y_recv, z_send, z_recv, moved, faces, t_fwd, t_gain, t_lam, t_lag,
+    (wide, wide_adj, state, lam, y_send, y_recv, z_send, z_recv, moved, faces, t_fwd, t_gain, t_lam, t_lag, weights,
      send_sem, recv_sem, in_sem) = refs
     fetches = [pltpu.make_async_copy(i, f, in_sem.at[k]) for k, (i, f) in enumerate(zip(inputs, fetched))]
     for k in (0, 2, 3, 4, 5, 1, 7, 8, 9, 10, 11, 6):
@@ -199,22 +207,42 @@
     for k in (7, 8, 9, 10, 11):
         fetches[k].wait()
     ka_row, kb_row = ka_ref[...], kb_ref[...]
-    ka_full = jnp.broadcast_to(ka_row, (bins, bins))
-    kb_full = jnp.broadcast_to(kb_row, (bins, bins))
-    ka_col, kb_col = ka_full.T, kb_full.T
-    pair = ka_col * kb_full + kb_col * ka_full
+    weights[0] = jnp.broadcast_to(ka_row, (bins, bins)).T
+    weights[1] = jnp.broadcast_to(kb_row, (bins, bins)).T
+    ka_col, kb_col = weights[0], weights[1]
+    first, corrected = 2 * PART, 4 * PART
     forward = fwd_ref[...]
-    t_fwd[0:2 * bins, :] = table3(forward * ka_row)
-    t_fwd[2 * bins:4 * bins, :] = table3(forward * kb_row)
-    t_fwd[4 * bins:, :] = table3(pair)
-    t_gain[...] = table3(gain_ref[...])
-    t_lam[...] = table3(forward)
+    ah, al = split(forward * ka_row)
+    bh, bl = split(forward * kb_row)
+    lh, ll = split(forward)
+    blank = jnp.zeros((PART, bins), BF16)
+    for c in range(bins // PART):
+        for q, high in enumerate((ah, bh)):
+            there = slice(c * corrected + q * first, c * corrected + (q + 1) * first)
+            t_fwd[there, :bins] = high[c * first:(c + 1) * first]
+            t_fwd[there, bins:] = high[c * first:(c + 1) * first]
+    sums, rest = 4 * bins, 4 * bins + PART
+    high, low = split(rows(ka_row, kb_row, jnp.zeros((PART - 2, bins), F32)))
+    t_fwd[sums:rest, :bins] = high
+    t_fwd[sums:rest, bins:] = high
+    t_fwd[rest:, :bins] = rows(al[:first], bl[:first], low)
+    t_fwd[rest:, bins:] = rows(*[blank] * 5)
+    t_lam[:2 * bins, :bins] = lh
+    t_lam[:2 * bins, bins:] = lh
+    t_lam[2 * bins:, :bins] = ll[:first]
+    t_lam[2 * bins:, bins:] = rows(blank, blank)
+    high, low = split(gain_ref[...])
+    t_gain[:, :2 * bins] = high
+    t_gain[:, 2 * bins:2 * bins + first] = high[:, :first]
+    t_gain[:, 2 * bins + first:] = low[:, :first]
     lag = lag_ref[...]
     ka_col2 = jnp.concatenate([ka_col, ka_col], axis=1)
     kb_col2 = jnp.concatenate([kb_col, kb_col], axis=1)
-    t_lag[:, :6 * bins] = table3(ka_col2 * lag)
-    t_lag[:, 6 * bins:12 * bins] = table3(kb_col2 * lag)
-    t_lag[:, 12 * bins:] = table3(-pair)
+    ah, al = split(ka_col2 * lag)
+    bh, bl = split(kb_col2 * lag)
+    t_lag[:, :2 * bins] = ah
+    t_lag[:, 2 * bins:4 * bins] = bh
+    t_lag[:, 4 * bins:] = jnp.concatenate([ah[:, :first], bh[:, :first], al[:, :first], bl[:, :first]], axis=1)
 
     fetches[1].wait()
     fetches[6].wait()
@@ -262,32 +290,49 @@
     def second_y(group):
         return y_copies(z_send.at[group], z_recv.at[group], 6 + 2 * group)
 
+    def coagulate(block):
+        beside = lambda values: jnp.concatenate(list(values), axis=1)
+        current = beside(moved[x] for x in block)
+        start = beside(lam[x + 1, :bins, :] for x in block)
+        ka = beside(weights[0] for _ in block)
+        kb = beside(weights[1] for _ in block)
+        saved = []
+        for step in range(SUBSTEPS):
+            high, low = split(current)
+            result = dot(t_fwd[...], rows(high, low))
+            spectra = [result[c:c + corrected] for c in range(0, sums, corrected)]
+            spectra[0] = spectra[0] + result[rest:rest + corrected]
+            spectra = [quarters(chunk) for chunk in spectra]
+            total_a, total_b = (
+                result[sums + k:sums + k + 1] + result[rest + corrected + k:rest + corrected + k + 1] for k in (0, 1))
+            loss = ka * total_b + kb * total_a
+            saved.append((spectra, loss))
+            if step < SUBSTEPS - 1:
+                high, low = high_low([product(*chunk) for chunk in spectra])
+                current = current + dot(t_gain[...], rows(*high, low, high[0])) - current * loss
+        adjoint = start
+        for step in reversed(range(SUBSTEPS)):
+            spectra, loss = saved[step]
+            high, low = split(adjoint)
+            result = dot(t_lam[...], rows(high, low))
+            spectra_l = [result[c:c + first] for c in range(0, 2 * bins, first)]
+            spectra_l[0] = spectra_l[0] + result[2 * bins:]
+            spectra_l = [quarters(chunk) for chunk in spectra_l]
+            high_b, low_b = high_low([product_conj(*l, *v[2:]) for l, v in zip(spectra_l, spectra)])
+            high_a, low_a = high_low([product_conj(*l, *v[:2]) for l, v in zip(spectra_l, spectra)])
+            terms = rows(*high_b, *high_a, low_b, low_a, high_b[0], high_a[0])
+            adjoint = adjoint + dot(t_lag[...], terms) - adjoint * loss
+        on = beside(active[pl.ds(x, 1), :] for x in block) == 1
+        result = jnp.where(on, adjoint, start)
+        for index, x in enumerate(block):
+            lam[x + 1, :bins, :] = result[:, index * width_y:(index + 1) * width_y]
+
     @pl.loop(0, 2)
     def _(group):
         places = [p + quarter * group for p in range(quarter)]
         places += [p + half - quarter * group for p in range(quarter, half)]
-        current = jnp.concatenate([moved[x] for x in places], axis=1)
-        start = jnp.concatenate([lam[x + 1, :bins, :] for x in places], axis=1)
-        saved = []
-        for step in range(SUBSTEPS):
-            spectra = dot(t_fwd[...], stacked(current))
-            loss = spectra[4 * bins:]
-            saved.append((current, spectra, loss))
-            if step < SUBSTEPS - 1:
-                both = product(spectra[:2 * bins], spectra[2 * bins:4 * bins])
-                current = current + dot(t_gain[...], stacked(both)) - current * loss
-        adjoint = start
-        for step in reversed(range(SUBSTEPS)):
-            current, spectra, loss = saved[step]
-            spectra_l = dot(t_lam[...], stacked(adjoint))
-            with_b = product_conj(spectra_l, spectra[2 * bins:4 * bins])
-            with_a = product_conj(spectra_l, spectra[:2 * bins])
-            terms = jnp.concatenate([stacked(with_b), stacked(with_a), stacked(adjoint * current)], axis=0)
-            adjoint = adjoint + dot(t_lag[...], terms) - adjoint * loss
-        on = jnp.concatenate([active[pl.ds(x, 1), :] for x in places], axis=1) == 1
-        result = jnp.where(on, adjoint, start)
-        for index, x in enumerate(places):
-            lam[x + 1, :bins, :] = result[:, index * width_y:(index + 1) * width_y]
+        for pick in range(0, half, BLOCK):
+            coagulate(places[pick:pick + BLOCK])
 
         @pl.when(group == 0)
         def _():
@@ -308,24 +353,24 @@
 
 def body(n_gx, n_gy, concentration, adjoint_next, sign_x, sign_y, courant_x, courant_y, active, kernel_a, kernel_b):
     bins, width_x, width_y = concentration.shape
-    rows = bins * width_x
+    cells = bins * width_x
     tables = dft_tables(bins)
     operands = (
-        concentration.reshape(rows, width_y),
-        adjoint_next.reshape(rows, width_y),
+        concentration.reshape(cells, width_y),
+        adjoint_next.reshape(cells, width_y),
         sign_x, sign_y, courant_x, courant_y, active,
         kernel_a.reshape(1, bins), kernel_b.reshape(1, bins),
         *(jnp.asarray(t) for t in tables),
     )
     result = pl.pallas_call(
         functools.partial(kernel, n_gx, n_gy, width_x),
-        out_shape=pltpu.VMEM((rows, width_y), F32),
+        out_shape=pltpu.VMEM((cells, width_y), F32),
         in_specs=[pl.BlockSpec(memory_space=pltpu.HBM)] * 12,
         out_specs=pl.BlockSpec(memory_space=pltpu.VMEM),
         scratch_shapes=[
             *(pltpu.VMEM(a.shape, a.dtype) for a in operands),
-            pltpu.VMEM((rows, width_y), F32),
-            pltpu.VMEM((rows, width_y), F32),
+            pltpu.VMEM((cells, width_y), F32),
+            pltpu.VMEM((cells, width_y), F32),
             pltpu.VMEM((width_x + 2, bins + 8, width_y), F32),
             pltpu.VMEM((width_x + 2, bins + 8, width_y), F32),
             pltpu.VMEM((2, bins + 2 * width_x, width_y), F32),
@@ -334,10 +379,11 @@
             pltpu.VMEM((2, 2, bins, width_y), F32),
             pltpu.VMEM((width_x, bins, width_y), F32),
             pltpu.VMEM((9, width_x, width_y), F32),
-            pltpu.VMEM((5 * bins, 3 * bins), BF16),
-            pltpu.VMEM((bins, 6 * bins), BF16),
-            pltpu.VMEM((2 * bins, 3 * bins), BF16),
-            pltpu.VMEM((bins, 15 * bins), BF16),
+            pltpu.VMEM((4 * bins + 6 * PART, 2 * bins), BF16),
+            pltpu.VMEM((bins, 2 * bins + 4 * PART), BF16),
+            pltpu.VMEM((2 * bins + 2 * PART, 2 * bins), BF16),
+            pltpu.VMEM((bins, 4 * bins + 8 * PART), BF16),
+            pltpu.VMEM((2, bins, bins), F32),
             pltpu.SemaphoreType.DMA((10,)),
             pltpu.SemaphoreType.DMA((10,)),
             pltpu.SemaphoreType.DMA((12,)),

time: 33.3 us -> 25.5 us (0.77)
  Pallas kernels: 32.2 us -> 24.4 us
    pallas_call x1, Pallas kernels: 32.2 us -> 24.4 us  [body(): pl.pallas_call(functools.partial(kernel, n_gx, n_gy, width_x), out_shape=...]
where the time goes in v1:
time: 25.5 us; the launch traced here: 25.4 us
  Pallas kernels  24.4 us (96%)
  local copies, waits for them, and re-layouts  0.97 us (4%)
    pallas_call x1, Pallas kernels, body(): pl.pallas_call(functools.partial(kernel, n_gx, n_gy, width_x), out_shape=...  24.4 us
    unnamed x1, local copies, waits for them, and re-layouts  0.97 us

profile of v1, /device:TPU:0, one launch (start us, length us, event | category | flops | bytes accessed | tf_op | source)
XLA Modules:
  0.0 25.4 jit_solution(7203555754493399976)
XLA Ops:
  0.0 24.4 %shard_map.118 = f32[2048,128]{1,0:T(8,128)S(1)} custom-call(bf16[2048,128]{1,0:T(8,128)(2,1)} %bitcast.6, bf16[2048,128]{1,0:T(8,128)(2,1)} %bitcast.7, s32[16,128]{1,0:T(8,128)} %refs_2_.1, s32[16,128]{1,0:T(8,128)} %refs_3_.1, f32[16,128]{1,0:T(8,128)} %refs_4_.1, f32[16,128]{1,0:T(8,128)} %refs_5_.1, s32[16,128]{1,0:T(8,128)} %refs_6_.1, ...), custom_call_target="tpu_custom_call" | custom-call | tf_op jit(solution)/shard_map/pallas_call | solution.py:365
  24.4 1.0 %copy.14 = f32[128,16,128]{2,1,0:T(8,128)} copy(f32[128,16,128]{2,1,0:T(8,128)S(1)} %bitcast.5) | data formatting | bytes 2097152

commit v2 on v1

--- a/solution.py
+++ b/solution.py
@@ -10,7 +10,8 @@
 
 SUBSTEPS = 4
 PART = 16
-BLOCK = 8
+EARLY = 8
+MIDDLE = 1
 F32 = jnp.float32
 BF16 = jnp.bfloat16
 
@@ -76,7 +77,7 @@
     out, refs = refs[0], refs[1:]
     fetched, refs = refs[:12], refs[12:]
     conc, adj, sx, sy, cx, cy, active, ka_ref, kb_ref, fwd_ref, gain_ref, lag_ref = fetched
-    (wide, wide_adj, state, lam, y_send, y_recv, z_send, z_recv, moved, faces, t_fwd, t_gain, t_lam, t_lag, weights,
+    (wide, wide_adj, state, lam, y_send, y_recv, z_send, z_recv, faces, t_fwd, t_gain, t_lam, t_lag, weights,
      send_sem, recv_sem, in_sem) = refs
     fetches = [pltpu.make_async_copy(i, f, in_sem.at[k]) for k, (i, f) in enumerate(zip(inputs, fetched))]
     for k in (0, 2, 3, 4, 5, 1, 7, 8, 9, 10, 11, 6):
@@ -102,8 +103,21 @@
     def _():
         pl.semaphore_signal(barrier, inc=1, device_id=(gx, nxt_y), device_id_type=mesh_id)
 
+    span = width_y // width_x
     lane = lax.broadcasted_iota(jnp.int32, (bins, width_y), 1)
+    owner, place = lane // span, lane % span
     lane_x = lax.broadcasted_iota(jnp.int32, (width_x, width_y), 1)
+    owner_x = lane_x // span
+
+    def pack(slab_of, owners):
+        packed = slab_of(0)
+        packed = pltpu.roll(packed, span // 2, 1)
+        for x in range(1, width_x):
+            packed = jnp.where(owners == x, pltpu.roll(slab_of(x), x * span + span // 2, 1), packed)
+        return packed
+
+    def unpack(packed, x):
+        return pltpu.roll(packed, width_y - x * span - span // 2, 1)
 
     for k in (2, 3, 4, 5):
         fetches[k].wait()
@@ -114,6 +128,21 @@
     bx = cx[...] * (1.0 - plus_x)
     uy = cy[...] * plus_y * inside
     by = cy[...] * (1.0 - plus_y) * inside
+
+    def put_faces(ux_after, bx_after, uy_last, by_last):
+        ux_next = rows(ux[1:], ux_after)
+        bx_next = rows(bx[1:], bx_after)
+        last_lane = lane_x == width_y - 1
+        uy_next = jnp.where(last_lane, uy_last, pltpu.roll(uy, width_y - 1, 1))
+        by_next = jnp.where(last_lane, by_last, pltpu.roll(by, width_y - 1, 1))
+        centre = 1.0 - bx - ux_next - by - uy_next
+        for index, values in enumerate((uy, by, ux, bx, ux_next, bx_next, uy_next, by_next, centre)):
+            for x in range(width_x):
+                faces[x, index:index + 1, :] = values[x:x + 1]
+
+    for x in range(width_x):
+        faces[x, 8:, :] = jnp.zeros((8, width_y), F32)
+    put_faces(ux[:1], bx[:1], uy, by)
 
     fetches[0].wait()
     wide[...] = conc[...].astype(F32)
@@ -143,28 +172,17 @@
     for x in range(1, width_x - 1):
         state[x + 1, :bins, :] = wide[pl.ds(x, bins, stride=width_x), :]
 
-    def edges(field, places):
-        to_prv = jnp.zeros((bins, width_y), F32)
-        to_nxt = jnp.zeros((bins, width_y), F32)
-        for x in places:
-            slab = field[x + 1, :bins, :]
-            to_prv = jnp.where(lane == x, pltpu.roll(slab, x, 1), to_prv)
-            to_nxt = jnp.where(lane == x, pltpu.roll(slab, x + 1, 1), to_nxt)
-        return to_prv, to_nxt
-
-    y_send[0, :bins, :], y_send[1, :bins, :] = edges(state, range(width_x))
-    y_send[0, bins:bins + width_x, :] = uy
-    y_send[0, bins + width_x:, :] = by
-    y_send[1, bins:, :] = jnp.zeros((2 * width_x, width_y), F32)
+    y_send[:bins, :] = pack(lambda x: state[x + 1, :bins, :], owner)
+    y_send[bins:, :] = pack(lambda x: faces[x, :8, :], owner[:8])
 
     def y_copies(source, target, base):
         return (
             pltpu.make_async_remote_copy(
-                src_ref=source.at[0], dst_ref=target.at[1],
+                src_ref=source, dst_ref=target.at[1],
                 send_sem=send_sem.at[base], recv_sem=recv_sem.at[base],
                 device_id=(gx, prv_y), device_id_type=mesh_id),
             pltpu.make_async_remote_copy(
-                src_ref=source.at[1], dst_ref=target.at[0],
+                src_ref=source, dst_ref=target.at[0],
                 send_sem=send_sem.at[base + 1], recv_sem=recv_sem.at[base + 1],
                 device_id=(gx, nxt_y), device_id_type=mesh_id),
         )
@@ -247,53 +265,35 @@
     fetches[1].wait()
     fetches[6].wait()
     wide_adj[...] = adj[...].astype(F32)
-    for x in range(width_x):
-        lam[x + 1, :bins, :] = wide_adj[pl.ds(x, bins, stride=width_x), :]
-
-    wait_y(first_y)
-    for copy in first_x:
-        copy.wait()
-
-    ux_next = jnp.concatenate([ux[1:], state[width_x + 1, bins:bins + 1, :]], axis=0)
-    bx_next = jnp.concatenate([bx[1:], state[width_x + 1, bins + 1:bins + 2, :]], axis=0)
-    last_lane = lane_x == width_y - 1
-    uy_next = jnp.where(
-        last_lane, pltpu.roll(y_recv[1, bins:bins + width_x, :], width_y - 1, 1), pltpu.roll(uy, width_y - 1, 1))
-    by_next = jnp.where(
-        last_lane, pltpu.roll(y_recv[1, bins + width_x:, :], width_y - 1, 1), pltpu.roll(by, width_y - 1, 1))
-    centre = 1.0 - bx - ux_next - by - uy_next
-    for index, values in enumerate((centre, ux, bx, ux_next, bx_next, uy, by, uy_next, by_next)):
-        faces[index] = values
-
-    def stencil(field, halo, x, low_x, high_x, low_y, high_y):
+    ending = lambda x: wide_adj[pl.ds(x, bins, stride=width_x), :]
+
+    def stencil(field, x, low_x, high_x, low_y, high_y):
         slab = field[x + 1, :bins, :]
-        before = jnp.where(lane == 0, pltpu.roll(halo[0, :bins, :], (width_y - x) % width_y, 1), pltpu.roll(slab, 1, 1))
-        after = jnp.where(
-            lane == width_y - 1, pltpu.roll(halo[1, :bins, :], width_y - 1 - x, 1), pltpu.roll(slab, width_y - 1, 1))
-        row = lambda k: faces[k, x:x + 1, :]
+        row = lambda k: faces[x, k:k + 1, :]
         return (
-            slab * row(0)
+            slab * row(8)
             + row(low_x) * field[x, :bins, :]
             + row(high_x) * field[x + 2, :bins, :]
-            + row(low_y) * before
-            + row(high_y) * after
+            + row(low_y) * pltpu.roll(slab, 1, 1)
+            + row(high_y) * pltpu.roll(slab, width_y - 1, 1)
         )
 
-    for x in range(width_x):
-        moved[x] = stencil(state, y_recv, x, 1, 4, 5, 8)
-
-    lam[1, bins:, :] = jnp.zeros((8, width_y), F32)
-    lam[width_x, bins:, :] = jnp.zeros((8, width_y), F32)
-    half, quarter = width_x // 2, width_x // 4
-    second_x = x_copies(lam, 4)
-
-    def second_y(group):
-        return y_copies(z_send.at[group], z_recv.at[group], 6 + 2 * group)
+    def packed_stencil(packed, rows_x, rows_y, low_x, high_x, low_y, high_y):
+        near = pack(lambda x: faces[x], owner[:16])
+        row = lambda k: near[k:k + 1]
+        x_before, x_after = rows_x
+        x_before = jnp.where(owner == 0, pltpu.roll(x_before, span // 2, 1), pltpu.roll(packed, span, 1))
+        x_after = jnp.where(
+            owner == width_x - 1, pltpu.roll(x_after, width_y - span // 2, 1), pltpu.roll(packed, width_y - span, 1))
+        y_before = pltpu.roll(jnp.where(place == span // 2 - 1, rows_y[0], packed), 1, 1)
+        y_after = pltpu.roll(jnp.where(place == span // 2, rows_y[1], packed), width_y - 1, 1)
+        return (packed * row(8) + row(low_x) * x_before + row(high_x) * x_after
+                + row(low_y) * y_before + row(high_y) * y_after)
 
     def coagulate(block):
         beside = lambda values: jnp.concatenate(list(values), axis=1)
-        current = beside(moved[x] for x in block)
-        start = beside(lam[x + 1, :bins, :] for x in block)
+        current = beside(cell[0] for cell in block)
+        start = beside(cell[1] for cell in block)
         ka = beside(weights[0] for _ in block)
         kb = beside(weights[1] for _ in block)
         saved = []
@@ -322,33 +322,60 @@
             high_a, low_a = high_low([product_conj(*l, *v[:2]) for l, v in zip(spectra_l, spectra)])
             terms = rows(*high_b, *high_a, low_b, low_a, high_b[0], high_a[0])
             adjoint = adjoint + dot(t_lag[...], terms) - adjoint * loss
-        on = beside(active[pl.ds(x, 1), :] for x in block) == 1
+        on = beside(cell[2] for cell in block) == 1
         result = jnp.where(on, adjoint, start)
-        for index, x in enumerate(block):
-            lam[x + 1, :bins, :] = result[:, index * width_y:(index + 1) * width_y]
-
-    @pl.loop(0, 2)
-    def _(group):
-        places = [p + quarter * group for p in range(quarter)]
-        places += [p + half - quarter * group for p in range(quarter, half)]
-        for pick in range(0, half, BLOCK):
-            coagulate(places[pick:pick + BLOCK])
-
-        @pl.when(group == 0)
-        def _():
-            for copy in second_x:
-                copy.start()
-
-        z_send[group, 0], z_send[group, 1] = edges(lam, places)
-        start_y(second_y(group), z_recv.at[group])
-
-    outer = [*range(quarter), *range(half + quarter, width_x)]
+        return [result[:, index * width_y:(index + 1) * width_y] for index in range(len(block))]
+
+    def cells_of(x):
+        return stencil(state, x, 2, 5, 0, 7), ending(x), active[pl.ds(x, 1), :]
+
+    def coagulate_rows(places):
+        for x, result in zip(places, coagulate([cells_of(x) for x in places])):
+            lam[x + 1] = result
+
+    early = range(1, 1 + EARLY)
+    beside_edges = range(1 + EARLY, 1 + EARLY + MIDDLE)
+    late = range(1 + EARLY + MIDDLE, width_x - 1)
+    packed_ending = pack(ending, owner)
+    packed_active = pack(lambda x: active[pl.ds(x, 1), :], owner[:1])
+    coagulate_rows(early)
+
+    wait_y(first_y)
+    for copy in first_x:
+        copy.wait()
+    uy_last = rows(*(unpack(y_recv[1, bins:bins + 1, :], x) for x in range(width_x)))
+    by_last = rows(*(unpack(y_recv[1, bins + 1:bins + 2, :], x) for x in range(width_x)))
+    uy_last = pltpu.roll(uy_last, width_y - 1, 1)
+    by_last = pltpu.roll(by_last, width_y - 1, 1)
+    put_faces(state[width_x + 1, bins:bins + 1, :], state[width_x + 1, bins + 1:bins + 2, :], uy_last, by_last)
+    packed = packed_stencil(
+        y_send[:bins, :], (state[0, :bins, :], state[width_x + 1, :bins, :]),
+        (y_recv[0, :bins, :], y_recv[1, :bins, :]), 2, 5, 0, 7)
+    ends = (0, width_x - 1)
+    results = coagulate(
+        [(packed, packed_ending, packed_active)] + [cells_of(x) for x in (*ends, *beside_edges)])
+    z_send[...] = results[0]
+    edge = (lane == 0) | (lane == width_y - 1)
+    for x, result in zip(ends, results[1:]):
+        lam[x + 1] = jnp.where(edge, unpack(results[0], x), result)
+    for x, result in zip(beside_edges, results[3:]):
+        lam[x + 1] = result
+    second_x = x_copies(lam, 4)
+    for copy in second_x:
+        copy.start()
+    second_y = y_copies(z_send, z_recv, 6)
+    start_y(second_y, z_recv)
+
+    coagulate_rows(late)
+
+    wait_y(second_y)
     for copy in second_x:
         copy.wait()
-    for group, places in enumerate((outer, range(quarter, half + quarter))):
-        wait_y(second_y(group))
-        for x in places:
-            out[pl.ds(x, bins, stride=width_x), :] = stencil(lam, z_recv.at[group], x, 2, 3, 6, 7)
+    packed = packed_stencil(z_send[...], (lam[0], lam[width_x + 1]), (z_recv[0], z_recv[1]), 3, 4, 1, 6)
+    near_edge = (lane < 2) | (lane >= width_y - 2)
+    for x in range(width_x):
+        out[pl.ds(x, bins, stride=width_x), :] = jnp.where(
+            near_edge, unpack(packed, x), stencil(lam, x, 3, 4, 1, 6))
 
 
 def body(n_gx, n_gy, concentration, adjoint_next, sign_x, sign_y, courant_x, courant_y, active, kernel_a, kernel_b):
@@ -372,20 +399,19 @@
             pltpu.VMEM((cells, width_y), F32),
             pltpu.VMEM((cells, width_y), F32),
             pltpu.VMEM((width_x + 2, bins + 8, width_y), F32),
-            pltpu.VMEM((width_x + 2, bins + 8, width_y), F32),
-            pltpu.VMEM((2, bins + 2 * width_x, width_y), F32),
-            pltpu.VMEM((2, bins + 2 * width_x, width_y), F32),
-            pltpu.VMEM((2, 2, bins, width_y), F32),
-            pltpu.VMEM((2, 2, bins, width_y), F32),
-            pltpu.VMEM((width_x, bins, width_y), F32),
-            pltpu.VMEM((9, width_x, width_y), F32),
+            pltpu.VMEM((width_x + 2, bins, width_y), F32),
+            pltpu.VMEM((bins + 8, width_y), F32),
+            pltpu.VMEM((2, bins + 8, width_y), F32),
+            pltpu.VMEM((bins, width_y), F32),
+            pltpu.VMEM((2, bins, width_y), F32),
+            pltpu.VMEM((width_x, 16, width_y), F32),
             pltpu.VMEM((4 * bins + 6 * PART, 2 * bins), BF16),
             pltpu.VMEM((bins, 2 * bins + 4 * PART), BF16),
             pltpu.VMEM((2 * bins + 2 * PART, 2 * bins), BF16),
             pltpu.VMEM((bins, 4 * bins + 8 * PART), BF16),
             pltpu.VMEM((2, bins, bins), F32),
-            pltpu.SemaphoreType.DMA((10,)),
-            pltpu.SemaphoreType.DMA((10,)),
+            pltpu.SemaphoreType.DMA((8,)),
+            pltpu.SemaphoreType.DMA((8,)),
             pltpu.SemaphoreType.DMA((12,)),
         ],
         compiler_params=pltpu.CompilerParams(

time: 25.5 us -> 20.3 us (0.80)
  Pallas kernels: 24.4 us -> 19.2 us
    pallas_call x1, Pallas kernels: 24.4 us -> 19.2 us  [body(): pl.pallas_call(functools.partial(kernel, n_gx, n_gy, width_x), out_shape=...]
where the time goes in v2:
time: 20.3 us; the launch traced here: 20.2 us
  Pallas kernels  19.2 us (95%)
  local copies, waits for them, and re-layouts  0.97 us (5%)
    pallas_call x1, Pallas kernels, body(): pl.pallas_call(functools.partial(kernel, n_gx, n_gy, width_x), out_shape=...  19.2 us
    unnamed x1, local copies, waits for them, and re-layouts  0.97 us

profile of v2, /device:TPU:0, one launch (start us, length us, event | category | flops | bytes accessed | tf_op | source)
XLA Modules:
  0.0 20.2 jit_solution(10859198841256740518)
XLA Ops:
  0.0 19.2 %shard_map.118 = f32[2048,128]{1,0:T(8,128)S(1)} custom-call(bf16[2048,128]{1,0:T(8,128)(2,1)} %bitcast.6, bf16[2048,128]{1,0:T(8,128)(2,1)} %bitcast.7, s32[16,128]{1,0:T(8,128)} %refs_2_.1, s32[16,128]{1,0:T(8,128)} %refs_3_.1, f32[16,128]{1,0:T(8,128)} %refs_4_.1, f32[16,128]{1,0:T(8,128)} %refs_5_.1, s32[16,128]{1,0:T(8,128)} %refs_6_.1, ...), custom_call_target="tpu_custom_call" | custom-call | tf_op jit(solution)/shard_map/pallas_call | solution.py:392
  19.2 1.0 %copy.14 = f32[128,16,128]{2,1,0:T(8,128)} copy(f32[128,16,128]{2,1,0:T(8,128)S(1)} %bitcast.5) | data formatting | bytes 2097152

commit v3 on v2

--- a/solution.py
+++ b/solution.py
@@ -10,8 +10,8 @@
 
 SUBSTEPS = 4
 PART = 16
-EARLY = 8
-MIDDLE = 1
+BEFORE = (6,)
+AFTER = (7,)
 F32 = jnp.float32
 BF16 = jnp.bfloat16
 
@@ -64,9 +64,13 @@
     return tuple(chunk[q * PART:(q + 1) * PART] for q in range(chunk.shape[0] // PART))
 
 
+def first_precise(chunks):
+    return [chunks[0], *(c.astype(BF16) for c in chunks[1:])]
+
+
 def high_low(chunks):
     high, low = split(chunks[0])
-    return [high, *(c.astype(BF16) for c in chunks[1:])], low
+    return [high, *chunks[1:]], low
 
 
 def kernel(
@@ -77,7 +81,7 @@
     out, refs = refs[0], refs[1:]
     fetched, refs = refs[:12], refs[12:]
     conc, adj, sx, sy, cx, cy, active, ka_ref, kb_ref, fwd_ref, gain_ref, lag_ref = fetched
-    (wide, wide_adj, state, lam, y_send, y_recv, z_send, z_recv, faces, t_fwd, t_gain, t_lam, t_lag, weights,
+    (wide, wide_adj, state, lam, y_send, y_recv, z_send, z_recv, own, faces, near, t_fwd, t_gain, t_lam, t_lag, weights,
      send_sem, recv_sem, in_sem) = refs
     fetches = [pltpu.make_async_copy(i, f, in_sem.at[k]) for k, (i, f) in enumerate(zip(inputs, fetched))]
     for k in (0, 2, 3, 4, 5, 1, 7, 8, 9, 10, 11, 6):
@@ -119,6 +123,20 @@
     def unpack(packed, x):
         return pltpu.roll(packed, width_y - x * span - span // 2, 1)
 
+    pieces = span // 2
+    depth = bins // pieces
+    shelf = ((place[:depth] + span - (pieces - 1)) % span) // 2
+
+    def thin(packed):
+        result = packed[:depth]
+        for piece in range(1, pieces):
+            part = pltpu.roll(packed[piece * depth:(piece + 1) * depth], 2 * piece, 1)
+            result = jnp.where(shelf == piece, part, result)
+        return result
+
+    def widen(thinned):
+        return rows(thinned, *(pltpu.roll(thinned, width_y - 2 * piece, 1) for piece in range(1, pieces)))
+
     for k in (2, 3, 4, 5):
         fetches[k].wait()
     plus_x = sx[...].astype(F32)
@@ -137,11 +155,9 @@
         by_next = jnp.where(last_lane, by_last, pltpu.roll(by, width_y - 1, 1))
         centre = 1.0 - bx - ux_next - by - uy_next
         for index, values in enumerate((uy, by, ux, bx, ux_next, bx_next, uy_next, by_next, centre)):
-            for x in range(width_x):
-                faces[x, index:index + 1, :] = values[x:x + 1]
-
-    for x in range(width_x):
-        faces[x, 8:, :] = jnp.zeros((8, width_y), F32)
+            faces[pl.ds(index, width_x, stride=16), :] = values
+
+    faces[...] = jnp.zeros(faces.shape, F32)
     put_faces(ux[:1], bx[:1], uy, by)
 
     fetches[0].wait()
@@ -172,8 +188,10 @@
     for x in range(1, width_x - 1):
         state[x + 1, :bins, :] = wide[pl.ds(x, bins, stride=width_x), :]
 
-    y_send[:bins, :] = pack(lambda x: state[x + 1, :bins, :], owner)
-    y_send[bins:, :] = pack(lambda x: faces[x, :8, :], owner[:8])
+    packed = pack(lambda x: state[x + 1, :bins, :], owner)
+    own[...] = packed
+    y_send[:depth, :] = thin(packed)
+    y_send[depth:, :] = pack(lambda x: faces[x * 16:x * 16 + 8, :], owner[:8])
 
     def y_copies(source, target, base):
         return (
@@ -269,7 +287,7 @@
 
     def stencil(field, x, low_x, high_x, low_y, high_y):
         slab = field[x + 1, :bins, :]
-        row = lambda k: faces[x, k:k + 1, :]
+        row = lambda k: faces[x * 16 + k:x * 16 + k + 1, :]
         return (
             slab * row(8)
             + row(low_x) * field[x, :bins, :]
@@ -279,8 +297,7 @@
         )
 
     def packed_stencil(packed, rows_x, rows_y, low_x, high_x, low_y, high_y):
-        near = pack(lambda x: faces[x], owner[:16])
-        row = lambda k: near[k:k + 1]
+        row = lambda k: near[k:k + 1, :]
         x_before, x_after = rows_x
         x_before = jnp.where(owner == 0, pltpu.roll(x_before, span // 2, 1), pltpu.roll(packed, span, 1))
         x_after = jnp.where(
@@ -290,19 +307,20 @@
         return (packed * row(8) + row(low_x) * x_before + row(high_x) * x_after
                 + row(low_y) * y_before + row(high_y) * y_after)
 
-    def coagulate(block):
-        beside = lambda values: jnp.concatenate(list(values), axis=1)
+    def beside(values):
+        return jnp.concatenate(list(values), axis=1)
+
+    def forward_steps(block, saved):
         current = beside(cell[0] for cell in block)
-        start = beside(cell[1] for cell in block)
         ka = beside(weights[0] for _ in block)
         kb = beside(weights[1] for _ in block)
-        saved = []
         for step in range(SUBSTEPS):
             high, low = split(current)
             result = dot(t_fwd[...], rows(high, low))
+            yield
             spectra = [result[c:c + corrected] for c in range(0, sums, corrected)]
             spectra[0] = spectra[0] + result[rest:rest + corrected]
-            spectra = [quarters(chunk) for chunk in spectra]
+            spectra = [quarters(chunk) for chunk in first_precise(spectra)]
             total_a, total_b = (
                 result[sums + k:sums + k + 1] + result[rest + corrected + k:rest + corrected + k + 1] for k in (0, 1))
             loss = ka * total_b + kb * total_a
@@ -310,77 +328,121 @@
             if step < SUBSTEPS - 1:
                 high, low = high_low([product(*chunk) for chunk in spectra])
                 current = current + dot(t_gain[...], rows(*high, low, high[0])) - current * loss
+            yield
+
+    def backward_steps(block, saved, results):
+        start = beside(cell[1] for cell in block)
         adjoint = start
-        for step in reversed(range(SUBSTEPS)):
-            spectra, loss = saved[step]
+        for spectra, loss in reversed(saved):
             high, low = split(adjoint)
             result = dot(t_lam[...], rows(high, low))
+            yield
             spectra_l = [result[c:c + first] for c in range(0, 2 * bins, first)]
             spectra_l[0] = spectra_l[0] + result[2 * bins:]
-            spectra_l = [quarters(chunk) for chunk in spectra_l]
+            spectra_l = [quarters(chunk) for chunk in first_precise(spectra_l)]
             high_b, low_b = high_low([product_conj(*l, *v[2:]) for l, v in zip(spectra_l, spectra)])
             high_a, low_a = high_low([product_conj(*l, *v[:2]) for l, v in zip(spectra_l, spectra)])
             terms = rows(*high_b, *high_a, low_b, low_a, high_b[0], high_a[0])
             adjoint = adjoint + dot(t_lag[...], terms) - adjoint * loss
+            yield
         on = beside(cell[2] for cell in block) == 1
         result = jnp.where(on, adjoint, start)
-        return [result[:, index * width_y:(index + 1) * width_y] for index in range(len(block))]
+        results += [result[:, index * width_y:(index + 1) * width_y] for index in range(len(block))]
+
+    def run(*phases):
+        phases = list(phases)
+        while phases:
+            phases = [phase for phase in phases if next(phase, phases) is None]
 
     def cells_of(x):
         return stencil(state, x, 2, 5, 0, 7), ending(x), active[pl.ds(x, 1), :]
 
-    def coagulate_rows(places):
-        for x, result in zip(places, coagulate([cells_of(x) for x in places])):
-            lam[x + 1] = result
-
-    early = range(1, 1 + EARLY)
-    beside_edges = range(1 + EARLY, 1 + EARLY + MIDDLE)
-    late = range(1 + EARLY + MIDDLE, width_x - 1)
+    class Group:
+        def __init__(self, places, extra=()):
+            self.places = places
+            self.cells = [*extra, *(cells_of(x) for x in places)]
+            self.saved, self.results = [], []
+
+        def forward(self):
+            return forward_steps(self.cells, self.saved)
+
+        def backward(self):
+            return backward_steps(self.cells, self.saved, self.results)
+
+        def put(self):
+            for x, result in zip(self.places, self.results):
+                lam[x + 1] = result
+
+    inner = iter(range(1, width_x - 1))
+    take = lambda count: [next(inner) for _ in range(count)]
+    ends = (0, width_x - 1)
+    previous = Group(take(BEFORE[0]))
+    run(previous.forward())
+    for count in BEFORE[1:]:
+        group = Group(take(count))
+        run(previous.backward(), group.forward())
+        previous.put()
+        previous = group
     packed_ending = pack(ending, owner)
     packed_active = pack(lambda x: active[pl.ds(x, 1), :], owner[:1])
-    coagulate_rows(early)
 
     wait_y(first_y)
     for copy in first_x:
         copy.wait()
-    uy_last = rows(*(unpack(y_recv[1, bins:bins + 1, :], x) for x in range(width_x)))
-    by_last = rows(*(unpack(y_recv[1, bins + 1:bins + 2, :], x) for x in range(width_x)))
+    uy_last = rows(*(unpack(y_recv[1, depth:depth + 1, :], x) for x in range(width_x)))
+    by_last = rows(*(unpack(y_recv[1, depth + 1:depth + 2, :], x) for x in range(width_x)))
     uy_last = pltpu.roll(uy_last, width_y - 1, 1)
     by_last = pltpu.roll(by_last, width_y - 1, 1)
     put_faces(state[width_x + 1, bins:bins + 1, :], state[width_x + 1, bins + 1:bins + 2, :], uy_last, by_last)
+    near[...] = pack(lambda x: faces[x * 16:(x + 1) * 16, :], owner[:16])
     packed = packed_stencil(
-        y_send[:bins, :], (state[0, :bins, :], state[width_x + 1, :bins, :]),
-        (y_recv[0, :bins, :], y_recv[1, :bins, :]), 2, 5, 0, 7)
-    ends = (0, width_x - 1)
-    results = coagulate(
-        [(packed, packed_ending, packed_active)] + [cells_of(x) for x in (*ends, *beside_edges)])
-    z_send[...] = results[0]
+        own[...], (state[0, :bins, :], state[width_x + 1, :bins, :]),
+        (widen(y_recv[0, :depth, :]), widen(y_recv[1, :depth, :])), 2, 5, 0, 7)
+    edges = Group([*ends, *take(width_x - 2 - sum(BEFORE) - sum(AFTER))], [(packed, packed_ending, packed_active)])
+    run(previous.backward(), edges.forward())
+    previous.put()
+    previous = Group(take(AFTER[0]))
+    run(edges.backward(), previous.forward())
+    packed, *edges.results = edges.results
+    own[...] = packed
+    z_send[...] = thin(packed)
     edge = (lane == 0) | (lane == width_y - 1)
-    for x, result in zip(ends, results[1:]):
-        lam[x + 1] = jnp.where(edge, unpack(results[0], x), result)
-    for x, result in zip(beside_edges, results[3:]):
-        lam[x + 1] = result
+    for k, x in enumerate(ends):
+        edges.results[k] = jnp.where(edge, unpack(packed, x), edges.results[k])
+    edges.put()
     second_x = x_copies(lam, 4)
     for copy in second_x:
         copy.start()
     second_y = y_copies(z_send, z_recv, 6)
     start_y(second_y, z_recv)
 
-    coagulate_rows(late)
+    for count in AFTER[1:]:
+        group = Group(take(count))
+        run(previous.backward(), group.forward())
+        previous.put()
+        previous = group
+    run(previous.backward())
+    previous.put()
+    for x in range(1, width_x - 1):
+        wide[x * bins:(x + 1) * bins, :] = stencil(lam, x, 3, 4, 1, 6)
 
     wait_y(second_y)
     for copy in second_x:
         copy.wait()
-    packed = packed_stencil(z_send[...], (lam[0], lam[width_x + 1]), (z_recv[0], z_recv[1]), 3, 4, 1, 6)
+    for x in ends:
+        wide[x * bins:(x + 1) * bins, :] = stencil(lam, x, 3, 4, 1, 6)
+    packed = packed_stencil(
+        own[...], (lam[0], lam[width_x + 1]), (widen(z_recv[0]), widen(z_recv[1])), 3, 4, 1, 6)
     near_edge = (lane < 2) | (lane >= width_y - 2)
     for x in range(width_x):
         out[pl.ds(x, bins, stride=width_x), :] = jnp.where(
-            near_edge, unpack(packed, x), stencil(lam, x, 3, 4, 1, 6))
+            near_edge, unpack(packed, x), wide[x * bins:(x + 1) * bins, :])
 
 
 def body(n_gx, n_gy, concentration, adjoint_next, sign_x, sign_y, courant_x, courant_y, active, kernel_a, kernel_b):
     bins, width_x, width_y = concentration.shape
     cells = bins * width_x
+    depth = bins * 2 * width_x // width_y
     tables = dft_tables(bins)
     operands = (
         concentration.reshape(cells, width_y),
@@ -400,11 +462,13 @@
             pltpu.VMEM((cells, width_y), F32),
             pltpu.VMEM((width_x + 2, bins + 8, width_y), F32),
             pltpu.VMEM((width_x + 2, bins, width_y), F32),
-            pltpu.VMEM((bins + 8, width_y), F32),
-            pltpu.VMEM((2, bins + 8, width_y), F32),
+            pltpu.VMEM((depth + 8, width_y), F32),
+            pltpu.VMEM((2, depth + 8, width_y), F32),
+            pltpu.VMEM((depth, width_y), F32),
+            pltpu.VMEM((2, depth, width_y), F32),
             pltpu.VMEM((bins, width_y), F32),
-            pltpu.VMEM((2, bins, width_y), F32),
-            pltpu.VMEM((width_x, 16, width_y), F32),
+            pltpu.VMEM((16 * width_x, width_y), F32),
+            pltpu.VMEM((16, width_y), F32),
             pltpu.VMEM((4 * bins + 6 * PART, 2 * bins), BF16),
             pltpu.VMEM((bins, 2 * bins + 4 * PART), BF16),
             pltpu.VMEM((2 * bins + 2 * PART, 2 * bins), BF16),

time: 20.3 us -> 18.2 us (0.90)
  Pallas kernels: 19.2 us -> 17.1 us
    pallas_call x1, Pallas kernels: 19.2 us -> 17.1 us  [body(): pl.pallas_call(functools.partial(kernel, n_gx, n_gy, width_x), out_shape=...]
where the time goes in v3:
time: 18.2 us; the launch traced here: 18.1 us
  Pallas kernels  17.1 us (94%)
  local copies, waits for them, and re-layouts  0.97 us (5%)
    pallas_call x1, Pallas kernels, body(): pl.pallas_call(functools.partial(kernel, n_gx, n_gy, width_x), out_shape=...  17.1 us
    unnamed x1, local copies, waits for them, and re-layouts  0.97 us

profile of v3, /device:TPU:0, one launch (start us, length us, event | category | flops | bytes accessed | tf_op | source)
XLA Modules:
  0.0 18.1 jit_solution(18428920549953047525)
XLA Ops:
  0.0 17.1 %shard_map.118 = f32[2048,128]{1,0:T(8,128)S(1)} custom-call(bf16[2048,128]{1,0:T(8,128)(2,1)} %bitcast.6, bf16[2048,128]{1,0:T(8,128)(2,1)} %bitcast.7, s32[16,128]{1,0:T(8,128)} %refs_2_.1, s32[16,128]{1,0:T(8,128)} %refs_3_.1, f32[16,128]{1,0:T(8,128)} %refs_4_.1, f32[16,128]{1,0:T(8,128)} %refs_5_.1, s32[16,128]{1,0:T(8,128)} %refs_6_.1, ...), custom_call_target="tpu_custom_call" | custom-call | tf_op jit(solution)/shard_map/pallas_call | solution.py:454
  17.1 1.0 %copy.14 = f32[128,16,128]{2,1,0:T(8,128)} copy(f32[128,16,128]{2,1,0:T(8,128)S(1)} %bitcast.5) | data formatting | bytes 2097152

commit v4 on v3

--- a/solution.py
+++ b/solution.py
@@ -10,8 +10,10 @@
 
 SUBSTEPS = 4
 PART = 16
-BEFORE = (6,)
-AFTER = (7,)
+BEFORE = 8
+AFTER = 6
+LEAD = 2
+BESIDE = 4
 F32 = jnp.float32
 BF16 = jnp.bfloat16
 
@@ -113,15 +115,37 @@
     lane_x = lax.broadcasted_iota(jnp.int32, (width_x, width_y), 1)
     owner_x = lane_x // span
 
+    def shift_of(x):
+        return (width_x - 1 - x) * span + span // 2
+
+    def pack_steps(slab_of, owners, results):
+        packed = pltpu.roll(slab_of(width_x - 1), span // 2, 1)
+        for x in range(width_x - 1):
+            packed = jnp.where(owners == width_x - 1 - x, pltpu.roll(slab_of(x), shift_of(x), 1), packed)
+            if x % 2:
+                yield
+        results.append(packed)
+
     def pack(slab_of, owners):
-        packed = slab_of(0)
-        packed = pltpu.roll(packed, span // 2, 1)
-        for x in range(1, width_x):
-            packed = jnp.where(owners == x, pltpu.roll(slab_of(x), x * span + span // 2, 1), packed)
-        return packed
+        results = []
+        run(pack_steps(slab_of, owners, results))
+        return results[0]
 
     def unpack(packed, x):
-        return pltpu.roll(packed, width_y - x * span - span // 2, 1)
+        return pltpu.roll(packed, width_y - shift_of(x), 1)
+
+    def run(steps, count=None):
+        if count is None:
+            for _ in steps:
+                pass
+        else:
+            for _ in range(count):
+                next(steps, None)
+
+    def weave(steps, others, count):
+        total = 2 * SUBSTEPS
+        for index, _ in enumerate(steps):
+            run(others, (index + 1) * count // total - index * count // total)
 
     pieces = span // 2
     depth = bins // pieces
@@ -299,9 +323,9 @@
     def packed_stencil(packed, rows_x, rows_y, low_x, high_x, low_y, high_y):
         row = lambda k: near[k:k + 1, :]
         x_before, x_after = rows_x
-        x_before = jnp.where(owner == 0, pltpu.roll(x_before, span // 2, 1), pltpu.roll(packed, span, 1))
-        x_after = jnp.where(
-            owner == width_x - 1, pltpu.roll(x_after, width_y - span // 2, 1), pltpu.roll(packed, width_y - span, 1))
+        x_before = jnp.where(
+            owner == width_x - 1, pltpu.roll(x_before, width_y - span // 2, 1), pltpu.roll(packed, width_y - span, 1))
+        x_after = jnp.where(owner == 0, pltpu.roll(x_after, span // 2, 1), pltpu.roll(packed, span, 1))
         y_before = pltpu.roll(jnp.where(place == span // 2 - 1, rows_y[0], packed), 1, 1)
         y_after = pltpu.roll(jnp.where(place == span // 2, rows_y[1], packed), width_y - 1, 1)
         return (packed * row(8) + row(low_x) * x_before + row(high_x) * x_after
@@ -349,18 +373,12 @@
         result = jnp.where(on, adjoint, start)
         results += [result[:, index * width_y:(index + 1) * width_y] for index in range(len(block))]
 
-    def run(*phases):
-        phases = list(phases)
-        while phases:
-            phases = [phase for phase in phases if next(phase, phases) is None]
-
     def cells_of(x):
         return stencil(state, x, 2, 5, 0, 7), ending(x), active[pl.ds(x, 1), :]
 
     class Group:
-        def __init__(self, places, extra=()):
-            self.places = places
-            self.cells = [*extra, *(cells_of(x) for x in places)]
+        def __init__(self, places, cells):
+            self.places, self.cells = places, cells
             self.saved, self.results = [], []
 
         def forward(self):
@@ -376,15 +394,24 @@
     inner = iter(range(1, width_x - 1))
     take = lambda count: [next(inner) for _ in range(count)]
     ends = (0, width_x - 1)
-    previous = Group(take(BEFORE[0]))
-    run(previous.forward())
-    for count in BEFORE[1:]:
-        group = Group(take(count))
-        run(previous.backward(), group.forward())
-        previous.put()
-        previous = group
-    packed_ending = pack(ending, owner)
+    places = take(BEFORE)
+    early = Group(places, [cells_of(x) for x in places])
+    middle_places = [*ends, *take(width_x - 2 - BEFORE - AFTER)]
+    late = Group(take(AFTER), [])
+    packed_ending = []
+
+    def prepare():
+        yield from pack_steps(ending, owner, packed_ending)
+        for x in late.places:
+            late.cells.append(cells_of(x))
+            yield
+
+    preparing = prepare()
+    weave(early.forward(), preparing, width_x // 2 + AFTER)
+    run(preparing)
     packed_active = pack(lambda x: active[pl.ds(x, 1), :], owner[:1])
+    early_steps = early.backward()
+    run(early_steps, LEAD)
 
     wait_y(first_y)
     for copy in first_x:
@@ -398,11 +425,13 @@
     packed = packed_stencil(
         own[...], (state[0, :bins, :], state[width_x + 1, :bins, :]),
         (widen(y_recv[0, :depth, :]), widen(y_recv[1, :depth, :])), 2, 5, 0, 7)
-    edges = Group([*ends, *take(width_x - 2 - sum(BEFORE) - sum(AFTER))], [(packed, packed_ending, packed_active)])
-    run(previous.backward(), edges.forward())
-    previous.put()
-    previous = Group(take(AFTER[0]))
-    run(edges.backward(), previous.forward())
+    edges = Group(
+        middle_places, [(packed, packed_ending[0], packed_active)] + [cells_of(x) for x in middle_places])
+    weave(edges.forward(), early_steps, 2 * SUBSTEPS - LEAD)
+    run(early_steps)
+    early.put()
+    late_steps = late.forward()
+    weave(edges.backward(), late_steps, BESIDE)
     packed, *edges.results = edges.results
     own[...] = packed
     z_send[...] = thin(packed)
@@ -416,27 +445,30 @@
     second_y = y_copies(z_send, z_recv, 6)
     start_y(second_y, z_recv)
 
-    for count in AFTER[1:]:
-        group = Group(take(count))
-        run(previous.backward(), group.forward())
-        previous.put()
-        previous = group
-    run(previous.backward())
-    previous.put()
-    for x in range(1, width_x - 1):
-        wide[x * bins:(x + 1) * bins, :] = stencil(lam, x, 3, 4, 1, 6)
+    def finish(places):
+        for x in places:
+            out[pl.ds(x, bins, stride=width_x), :] = stencil(lam, x, 3, 4, 1, 6)
+            yield
+
+    run(late_steps)
+    weave(late.backward(), finish(range(1, BEFORE)), BEFORE - 1)
+    late.put()
+    run(finish(range(BEFORE, width_x - 1)))
 
     wait_y(second_y)
     for copy in second_x:
         copy.wait()
-    for x in ends:
-        wide[x * bins:(x + 1) * bins, :] = stencil(lam, x, 3, 4, 1, 6)
+    run(finish(ends))
     packed = packed_stencil(
         own[...], (lam[0], lam[width_x + 1]), (widen(z_recv[0]), widen(z_recv[1])), 3, 4, 1, 6)
-    near_edge = (lane < 2) | (lane >= width_y - 2)
-    for x in range(width_x):
-        out[pl.ds(x, bins, stride=width_x), :] = jnp.where(
-            near_edge, unpack(packed, x), wide[x * bins:(x + 1) * bins, :])
+    own[...] = packed
+    near_edge = ((lane < 2) | (lane >= width_y - 2))[:8]
+    for b in range(bins):
+        for x in range(0, width_x, 8):
+            here = slice(b * width_x + x, b * width_x + x + 8)
+            cells = jnp.broadcast_to(own[b:b + 1, :], (8, width_y))
+            cells = pltpu.roll(cells, width_y - shift_of(x), 1, stride=span, stride_axis=0)
+            out[here, :] = jnp.where(near_edge, cells, out[here, :])
 
 
 def body(n_gx, n_gy, concentration, adjoint_next, sign_x, sign_y, courant_x, courant_y, active, kernel_a, kernel_b):

time: 18.2 us -> 17.8 us (0.978)
  Pallas kernels: 17.1 us -> 16.7 us
    pallas_call x1, Pallas kernels: 17.1 us -> 16.7 us  [body(): pl.pallas_call(functools.partial(kernel, n_gx, n_gy, width_x), out_shape=...]
where the time goes in v4:
time: 17.8 us; the launch traced here: 17.7 us
  Pallas kernels  16.7 us (94%)
  local copies, waits for them, and re-layouts  0.97 us (5%)
    pallas_call x1, Pallas kernels, body(): pl.pallas_call(functools.partial(kernel, n_gx, n_gy, width_x), out_shape=...  16.7 us
    unnamed x1, local copies, waits for them, and re-layouts  0.97 us

profile of v4, /device:TPU:0, one launch (start us, length us, event | category | flops | bytes accessed | tf_op | source)
XLA Modules:
  0.0 17.7 jit_solution(13891967926551306771)
XLA Ops:
  0.0 16.7 %shard_map.118 = f32[2048,128]{1,0:T(8,128)S(1)} custom-call(bf16[2048,128]{1,0:T(8,128)(2,1)} %bitcast.6, bf16[2048,128]{1,0:T(8,128)(2,1)} %bitcast.7, s32[16,128]{1,0:T(8,128)} %refs_2_.1, s32[16,128]{1,0:T(8,128)} %refs_3_.1, f32[16,128]{1,0:T(8,128)} %refs_4_.1, f32[16,128]{1,0:T(8,128)} %refs_5_.1, s32[16,128]{1,0:T(8,128)} %refs_6_.1, ...), custom_call_target="tpu_custom_call" | custom-call | tf_op jit(solution)/shard_map/pallas_call | solution.py:486
  16.7 1.0 %copy.14 = f32[128,16,128]{2,1,0:T(8,128)} copy(f32[128,16,128]{2,1,0:T(8,128)S(1)} %bitcast.5) | data formatting | bytes 2097152

commit v5 on v4

--- a/solution.py
+++ b/solution.py
@@ -12,7 +12,7 @@
 PART = 16
 BEFORE = 8
 AFTER = 6
-LEAD = 2
+LEAD = 0
 BESIDE = 4
 F32 = jnp.float32
 BF16 = jnp.bfloat16
@@ -144,8 +144,10 @@
 
     def weave(steps, others, count):
         total = 2 * SUBSTEPS
-        for index, _ in enumerate(steps):
+        for index in range(total):
             run(others, (index + 1) * count // total - index * count // total)
+            run(steps, 1)
+        run(steps)
 
     pieces = span // 2
     depth = bins // pieces
@@ -171,18 +173,12 @@
     uy = cy[...] * plus_y * inside
     by = cy[...] * (1.0 - plus_y) * inside
 
-    def put_faces(ux_after, bx_after, uy_last, by_last):
-        ux_next = rows(ux[1:], ux_after)
-        bx_next = rows(bx[1:], bx_after)
-        last_lane = lane_x == width_y - 1
-        uy_next = jnp.where(last_lane, uy_last, pltpu.roll(uy, width_y - 1, 1))
-        by_next = jnp.where(last_lane, by_last, pltpu.roll(by, width_y - 1, 1))
-        centre = 1.0 - bx - ux_next - by - uy_next
-        for index, values in enumerate((uy, by, ux, bx, ux_next, bx_next, uy_next, by_next, centre)):
-            faces[pl.ds(index, width_x, stride=16), :] = values
-
+    ux_next, bx_next = (rows(v[1:], v[:1]) for v in (ux, bx))
+    uy_next, by_next = (pltpu.roll(v, width_y - 1, 1) for v in (uy, by))
+    centre = 1.0 - bx - ux_next - by - uy_next
     faces[...] = jnp.zeros(faces.shape, F32)
-    put_faces(ux[:1], bx[:1], uy, by)
+    for index, values in enumerate((uy, by, ux, bx, ux_next, bx_next, uy_next, by_next, centre)):
+        faces[pl.ds(index, width_x, stride=16), :] = values
 
     fetches[0].wait()
     wide[...] = conc[...].astype(F32)
@@ -212,7 +208,7 @@
     for x in range(1, width_x - 1):
         state[x + 1, :bins, :] = wide[pl.ds(x, bins, stride=width_x), :]
 
-    packed = pack(lambda x: state[x + 1, :bins, :], owner)
+    packed = pack(lambda x: state[x + 1, :bins, :].astype(BF16), owner).astype(F32)
     own[...] = packed
     y_send[:depth, :] = thin(packed)
     y_send[depth:, :] = pack(lambda x: faces[x * 16:x * 16 + 8, :], owner[:8])
@@ -282,11 +278,12 @@
             t_fwd[there, :bins] = high[c * first:(c + 1) * first]
             t_fwd[there, bins:] = high[c * first:(c + 1) * first]
     sums, rest = 4 * bins, 4 * bins + PART
-    high, low = split(rows(ka_row, kb_row, jnp.zeros((PART - 2, bins), F32)))
-    t_fwd[sums:rest, :bins] = high
-    t_fwd[sums:rest, bins:] = high
-    t_fwd[rest:, :bins] = rows(al[:first], bl[:first], low)
-    t_fwd[rest:, bins:] = rows(*[blank] * 5)
+    empty = jnp.zeros((PART - 4, bins), F32)
+    high, low = ((v.astype(F32)) for v in split(rows(ka_row, kb_row)))
+    t_fwd[sums:rest, :bins] = rows(high, low, empty).astype(BF16)
+    t_fwd[sums:rest, bins:] = rows(high, 0.0 * low, empty).astype(BF16)
+    t_fwd[rest:, :bins] = rows(al[:first], bl[:first])
+    t_fwd[rest:, bins:] = rows(*[blank] * 4)
     t_lam[:2 * bins, :bins] = lh
     t_lam[:2 * bins, bins:] = lh
     t_lam[2 * bins:, :bins] = ll[:first]
@@ -346,7 +343,7 @@
             spectra[0] = spectra[0] + result[rest:rest + corrected]
             spectra = [quarters(chunk) for chunk in first_precise(spectra)]
             total_a, total_b = (
-                result[sums + k:sums + k + 1] + result[rest + corrected + k:rest + corrected + k + 1] for k in (0, 1))
+                result[sums + k:sums + k + 1] + result[sums + 2 + k:sums + 3 + k] for k in (0, 1))
             loss = ka * total_b + kb * total_a
             saved.append((spectra, loss))
             if step < SUBSTEPS - 1:
@@ -398,16 +395,19 @@
     early = Group(places, [cells_of(x) for x in places])
     middle_places = [*ends, *take(width_x - 2 - BEFORE - AFTER)]
     late = Group(take(AFTER), [])
-    packed_ending = []
+    packed_ending, near_faces = [], []
+    last = 16 * (width_x - 1)
 
     def prepare():
+        yield from pack_steps(lambda x: faces[x * 16:(x + 1) * 16, :], owner[:16], near_faces)
+        near[...] = near_faces[0]
         yield from pack_steps(ending, owner, packed_ending)
         for x in late.places:
             late.cells.append(cells_of(x))
             yield
 
     preparing = prepare()
-    weave(early.forward(), preparing, width_x // 2 + AFTER)
+    weave(early.forward(), preparing, width_x + AFTER)
     run(preparing)
     packed_active = pack(lambda x: active[pl.ds(x, 1), :], owner[:1])
     early_steps = early.backward()
@@ -416,12 +416,16 @@
     wait_y(first_y)
     for copy in first_x:
         copy.wait()
-    uy_last = rows(*(unpack(y_recv[1, depth:depth + 1, :], x) for x in range(width_x)))
-    by_last = rows(*(unpack(y_recv[1, depth + 1:depth + 2, :], x) for x in range(width_x)))
-    uy_last = pltpu.roll(uy_last, width_y - 1, 1)
-    by_last = pltpu.roll(by_last, width_y - 1, 1)
-    put_faces(state[width_x + 1, bins:bins + 1, :], state[width_x + 1, bins + 1:bins + 2, :], uy_last, by_last)
-    near[...] = pack(lambda x: faces[x * 16:(x + 1) * 16, :], owner[:16])
+    y_faces = pltpu.roll(y_recv[1, depth:, :], width_y - 1, 1)
+    x_faces = pltpu.roll(state[width_x + 1, bins:, :], span // 2, 1)
+    edge_faces = near_faces[0]
+    for k in (0, 1):
+        near[4 + k:5 + k, :] = jnp.where(owner[:1] == 0, x_faces[k:k + 1], edge_faces[4 + k:5 + k])
+        near[6 + k:7 + k, :] = jnp.where(place[:1] == span // 2 - 1, y_faces[k:k + 1], edge_faces[6 + k:7 + k])
+        faces[last + 4 + k:last + 5 + k, :] = state[width_x + 1, bins + k:bins + k + 1, :]
+    near[8:9, :] = 1.0 - near[3:4, :] - near[4:5, :] - near[1:2, :] - near[6:7, :]
+    faces[last + 8:last + 9, :] = (1.0 - faces[last + 3:last + 4, :] - faces[last + 4:last + 5, :]
+                                   - faces[last + 1:last + 2, :] - faces[last + 6:last + 7, :])
     packed = packed_stencil(
         own[...], (state[0, :bins, :], state[width_x + 1, :bins, :]),
         (widen(y_recv[0, :depth, :]), widen(y_recv[1, :depth, :])), 2, 5, 0, 7)
@@ -439,11 +443,11 @@
     for k, x in enumerate(ends):
         edges.results[k] = jnp.where(edge, unpack(packed, x), edges.results[k])
     edges.put()
+    second_y = y_copies(z_send, z_recv, 6)
+    start_y(second_y, z_recv)
     second_x = x_copies(lam, 4)
     for copy in second_x:
         copy.start()
-    second_y = y_copies(z_send, z_recv, 6)
-    start_y(second_y, z_recv)
 
     def finish(places):
         for x in places:
@@ -501,7 +505,7 @@
             pltpu.VMEM((bins, width_y), F32),
             pltpu.VMEM((16 * width_x, width_y), F32),
             pltpu.VMEM((16, width_y), F32),
-            pltpu.VMEM((4 * bins + 6 * PART, 2 * bins), BF16),
+            pltpu.VMEM((4 * bins + 5 * PART, 2 * bins), BF16),
             pltpu.VMEM((bins, 2 * bins + 4 * PART), BF16),
             pltpu.VMEM((2 * bins + 2 * PART, 2 * bins), BF16),
             pltpu.VMEM((bins, 4 * bins + 8 * PART), BF16),

time: 17.8 us -> 17.1 us (0.961)
  Pallas kernels: 16.7 us -> 15.9 us
    pallas_call x1, Pallas kernels: 16.7 us -> 15.9 us  [body(): pl.pallas_call(functools.partial(kernel, n_gx, n_gy, width_x), out_shape=...]
where the time goes in v5:
time: 17.1 us; the launch traced here: 16.9 us
  Pallas kernels  15.9 us (93%)
  local copies, waits for them, and re-layouts  0.97 us (6%)
    pallas_call x1, Pallas kernels, body(): pl.pallas_call(functools.partial(kernel, n_gx, n_gy, width_x), out_shape=...  15.9 us
    unnamed x1, local copies, waits for them, and re-layouts  0.97 us

profile of v5, /device:TPU:0, one launch (start us, length us, event | category | flops | bytes accessed | tf_op | source)
XLA Modules:
  0.0 16.9 jit_solution(16323903505262285535)
XLA Ops:
  0.0 15.9 %shard_map.118 = f32[2048,128]{1,0:T(8,128)S(1)} custom-call(bf16[2048,128]{1,0:T(8,128)(2,1)} %bitcast.6, bf16[2048,128]{1,0:T(8,128)(2,1)} %bitcast.7, s32[16,128]{1,0:T(8,128)} %refs_2_.1, s32[16,128]{1,0:T(8,128)} %refs_3_.1, f32[16,128]{1,0:T(8,128)} %refs_4_.1, f32[16,128]{1,0:T(8,128)} %refs_5_.1, s32[16,128]{1,0:T(8,128)} %refs_6_.1, ...), custom_call_target="tpu_custom_call" | custom-call | tf_op jit(solution)/shard_map/pallas_call | solution.py:490
  16.0 1.0 %copy.14 = f32[128,16,128]{2,1,0:T(8,128)} copy(f32[128,16,128]{2,1,0:T(8,128)S(1)} %bitcast.5) | data formatting | bytes 2097152

commit v6 on v5

--- a/solution.py
+++ b/solution.py
@@ -454,8 +454,10 @@
             out[pl.ds(x, bins, stride=width_x), :] = stencil(lam, x, 3, 4, 1, 6)
             yield
 
-    run(late_steps)
-    weave(late.backward(), finish(range(1, BEFORE)), BEFORE - 1)
+    finishing = finish(range(1, BEFORE))
+    weave(late_steps, finishing, BEFORE - 1)
+    run(finishing)
+    run(late.backward())
     late.put()
     run(finish(range(BEFORE, width_x - 1)))
 

time: 17.1 us -> 17.1 us (level)
  no operation moved by 1% of the time
where the time goes in v6:
time: 17.1 us; the launch traced here: 16.9 us
  Pallas kernels  15.9 us (93%)
  local copies, waits for them, and re-layouts  0.97 us (6%)
    pallas_call x1, Pallas kernels, body(): pl.pallas_call(functools.partial(kernel, n_gx, n_gy, width_x), out_shape=...  15.9 us
    unnamed x1, local copies, waits for them, and re-layouts  0.97 us

profile of v6, /device:TPU:0, one launch (start us, length us, event | category | flops | bytes accessed | tf_op | source)
XLA Modules:
  0.0 16.9 jit_solution(10684171871793082625)
XLA Ops:
  0.0 15.9 %shard_map.118 = f32[2048,128]{1,0:T(8,128)S(1)} custom-call(bf16[2048,128]{1,0:T(8,128)(2,1)} %bitcast.6, bf16[2048,128]{1,0:T(8,128)(2,1)} %bitcast.7, s32[16,128]{1,0:T(8,128)} %refs_2_.1, s32[16,128]{1,0:T(8,128)} %refs_3_.1, f32[16,128]{1,0:T(8,128)} %refs_4_.1, f32[16,128]{1,0:T(8,128)} %refs_5_.1, s32[16,128]{1,0:T(8,128)} %refs_6_.1, ...), custom_call_target="tpu_custom_call" | custom-call | tf_op jit(solution)/shard_map/pallas_call | solution.py:492
  16.0 1.0 %copy.14 = f32[128,16,128]{2,1,0:T(8,128)} copy(f32[128,16,128]{2,1,0:T(8,128)S(1)} %bitcast.5) | data formatting | bytes 2097152
